TPU v7x, 32 devices: a whole 2x2x4 slice. The times are simulated.
32 devices in a mesh: seg: 8 (over z, y), grp: 4 (over x, core).
Axes of the slice: x: 2, y: 2, z: 4, core: 2. Of those that a mesh axis runs over, the one named last changes fastest.
Arguments:
- spectra: bfloat16 [8, 2, 128, 12288], P(None, None, None, ('seg', 'grp'))
- band_bins: int32 [2, 2], replicated, may hold values from 0 to 80, as said below
- far_list: int32 [4, 8, 8, 4, 3], P('grp'), may hold values from 0 to 2, as said below
- far_count: int32 [4, 8, 8], P('grp'), may hold values from 0 to 4, as said below
Outputs:
- near_corr: bfloat16 [2, 2, 12288, 1536], P(None, None, ('seg', 'grp'))
- far_corr: bfloat16 [8, 4, 8, 4, 2, 128, 128], P('seg', 'grp')
Inputs may be any that keep to these rules, and one draw needn't show every extreme that they name: band_bins[b, 0] + 48 <= 128 and 1 <= band_bins[b, 1] <= 48; band 0 has exactly 48 bins; one band starts at bin 0 and the other at bin 128 - 48. far_list entries: row and column blocks 0 to 2, band 0 or 1. far_count is 0 where owner and source group are the same; every owner has some source group with exactly 4.
All inputs are finite; a program needn't handle non-finite values.
Results may differ from a plain program's by a relative error of at most 0.0058.
Values may be sent and summed in bfloat16 or wider, within the bound.
A program may use at most 192 MiB of HBM per device.

v0:
```python
import jax
import jax.numpy as jnp
from jax import lax
from jax.sharding import PartitionSpec as P

W = 8
F = 128
BAND_MAX = 48
SMOOTH = 4
BLOCK = 128
BLK_DEV = 3


HIGH = lax.Precision.HIGHEST


def whiten(spectra):
    values = spectra.astype(jnp.float32)
    power = jnp.sum(values * values, axis=(0, 1))
    bins = jnp.arange(F)
    window = (jnp.abs(bins[:, None] - bins[None, :]) <= SMOOTH).astype(jnp.float32)
    totals = jnp.sum(window, axis=1) * W
    level = (
        jnp.dot(window, power, precision=HIGH, preferred_element_type=jnp.float32) / totals[:, None]
    )
    return (values * lax.rsqrt(level + 1e-06)[None, None]).astype(jnp.bfloat16)


def band_operands(white, band_bins):
    cols = []
    ops = []
    for band in range(2):
        piece = lax.dynamic_slice_in_dim(white, band_bins[band, 0], BAND_MAX, 2)
        live = (jnp.arange(BAND_MAX) < band_bins[band, 1]).astype(jnp.bfloat16)
        rows = piece * live[None, None, :, None]
        twisted = jnp.stack([rows[:, 1], -rows[:, 0]], axis=1)
        cols.append(piece)
        ops.append(jnp.stack([rows, twisted], axis=0))
    scales = lax.rsqrt((W * band_bins[:, 1]).astype(jnp.float32))
    return (jnp.stack(cols), jnp.stack(ops), scales)


def body(spectra, band_bins, far_list, far_count):
    white = whiten(spectra)
    band_cols, row_ops, scales = band_operands(white, band_bins)
    piece = lax.all_gather(white, "grp", axis=3, tiled=True)
    results = []
    for band in range(2):
        cut = lax.dynamic_slice_in_dim(piece, band_bins[band, 0], BAND_MAX, 2)
        prod = jnp.einsum("owpfr,wpfk->ork", row_ops[band], cut, preferred_element_type=jnp.float32)
        results.append((prod * scales[band]).astype(jnp.bfloat16))
    near_corr = jnp.stack(results)
    seg_index = lax.axis_index("seg")
    lists = far_list[0]
    table = far_count[0]
    slots = lists.shape[2]
    slot_ids = jnp.arange(slots)
    sent = lax.dynamic_index_in_dim(lists, seg_index, 1, keepdims=False)
    sent_count = lax.dynamic_index_in_dim(table, seg_index, 1, keepdims=False)
    sent_live = (slot_ids[None, :] < sent_count[:, None]).astype(jnp.bfloat16)
    blocks = band_cols.reshape(2, W, 2, BAND_MAX, BLK_DEV, BLOCK)
    taken = lax.dynamic_index_in_dim(lists, seg_index, 0, keepdims=False)
    taken_count = lax.dynamic_index_in_dim(table, seg_index, 0, keepdims=False)
    payload = (
        blocks[sent[..., 2], :, :, :, sent[..., 1], :] * sent_live[:, :, None, None, None, None]
    )
    arrived = lax.all_to_all(payload, "seg", split_axis=0, concat_axis=0, tiled=True)
    taken_live = (slot_ids[None, :] < taken_count[:, None]).astype(jnp.float32)
    op_blocks = row_ops.reshape(2, 2, W, 2, BAND_MAX, BLK_DEV, BLOCK)
    chosen = op_blocks[taken[..., 2], :, :, :, :, taken[..., 0], :]
    prod = jnp.einsum("scowpfr,scwpfk->scork", chosen, arrived, preferred_element_type=jnp.float32)
    factor = scales[taken[..., 2]] * taken_live
    far_corr = (prod * factor[:, :, None, None, None]).astype(jnp.bfloat16)[None, None]
    return (near_corr, far_corr)


def solution(mesh):
    placed = (
        P(None, None, None, ("seg", "grp")),
        P(),
        P("grp", None, None, None, None),
        P("grp", None, None),
    )
    return jax.shard_map(
        body,
        mesh=mesh,
        in_specs=placed,
        out_specs=(
            P(None, None, ("seg", "grp"), None),
            P("seg", "grp", None, None, None, None, None),
        ),
        check_vma=False,
    )
```

profile of v0, /device:TPU:0, one launch (start us, length us, event | category | flops | bytes accessed | tf_op | source)
XLA Modules:
  0.0 198.1 jit_solution(16607002839730382438)
XLA Ops:
  7.2 0.0 copy-start
  7.2 0.0 copy-start.3
  7.2 0.0 all-gather.2.cloned.1.call-start
  7.2 0.1 convert_reduce_fusion
  7.4 1.9 fusion.6
  9.2 0.3 fusion.30
  9.5 0.0 copy-done.3
  9.5 0.0 copy-start.6
  9.5 0.0 copy-start.7
  9.5 1.5 fusion.7
  11.1 0.0 all-gather.2.cloned.1.call-update
  11.1 0.0 copy-done.6
  11.1 0.6 fusion.53
  14.2 0.0 copy-done.7
  14.2 0.2 dynamic-slice_reduce_fusion
  14.4 0.1 fusion.32
  14.5 0.7 compare_convert_fusion.1
  15.1 0.6 compare_convert_fusion
  15.8 0.0 copy-done
  15.8 0.1 constant_dynamic-slice_fusion.1
  15.9 0.1 copy.47
  16.0 0.1 copy.48
  16.1 0.1 reshape.110
  17.5 0.0 copy-done.2
  17.5 1.6 broadcast_multiply_fusion.2
  19.1 2.2 %reshape.135 = bf16[1,8,2,48,3,128]{5,4,3,1,2,0:T(4,128)(2,1)S(1)} reshape(bf16[8,2,48,384]{3,2,0,1:T(8,128)(2,1)} %get-tuple-element.3) | data formatting | bytes 1179648 | tf_op jit(solution)/shard_map/stack | solution.py:40
  21.3 0.9 copy.45
  22.2 0.2 reshape.136
  22.4 0.1 copy.46
  22.5 1.3 pad_maximum_fusion.1
  23.7 4.0 %gather_fusion.1 = bf16[32,8,2,48,128]{4,3,2,1,0:T(8,128)(2,1)} fusion(bf16[2,8,2,48,3,128]{5,3,4,2,1,0:T(8,128)(2,1)S(1)} %pad_maximum_fusion.1, s32[32]{0:T(128)S(1)} %reshape.110), kind=kCustom, calls=%fused_computation.1 | custom fusion | bytes 12583168 | tf_op jit(solution)/shard_map/gather | solution.py:65
  27.7 4.4 %copy.49 = bf16[32,8,2,48,128]{4,3,1,2,0:T(8,128)(2,1)S(1)} copy(bf16[32,8,2,48,128]{4,3,2,1,0:T(8,128)(2,1)} %gather_fusion.1) | data formatting | bytes 12582912 | tf_op jit(solution)/shard_map/gather | solution.py:65
  32.1 3.2 %broadcast_multiply_fusion = bf16[8,4,8,2,48,128]{5,4,2,3,1,0:T(8,128)(2,1)} fusion(bf16[8,4,8,2,48,128]{5,4,2,3,1,0:T(8,128)(2,1)S(1)} %bitcast.107, bf16[8,4]{1,0:T(8,128)(2,1)S(1)} %fusion.32), kind=kLoop, calls=%fused_computation.17 | loop fusion | flops 3145728 | bytes 12582976 | tf_op jit(solution)/shard_map/mul | solution.py:65
  35.3 7.4 %all-to-all-start = ((bf16[8,4,8,2,48,128]{5,4,2,3,1,0:T(8,128)(2,1)}), bf16[8,4,8,2,48,128]{5,4,2,3,1,0:T(8,128)(2,1)}, u32[]{:S(2)}, u32[]{:S(2)}) async-start(bf16[8,4,8,2,48,128]{5,4,2,3,1,0:T(8,128)(2,1)} %broadcast_multiply_fusion), calls=%async_computation | async-start | bytes 12582912 | tf_op jit(solution)/shard_map/all_to_all | solution.py:67
  42.7 0.1 copy.42
  42.8 0.1 reshape.104
  42.8 0.1 copy.51
  42.9 0.1 reshape.118
  43.0 0.2 fusion.48
  43.2 0.7 gather_fusion.2
  43.9 0.1 reshape.117
  44.0 0.2 reshape.131
  44.2 0.9 copy.36
  45.1 0.2 reshape.133
  45.3 0.9 copy.40
  46.2 0.0 copy-done.4
  46.2 0.1 fusion.51
  46.3 1.0 pad_maximum_fusion.2
  47.3 0.2 reshape.132
  47.5 0.9 copy.37
  48.4 0.9 pad_maximum_fusion.3
  49.3 0.2 reshape.134
  49.5 0.1 copy.41
  49.6 1.6 maximum_maximum_fusion
  51.2 6.9 %gather_fusion = bf16[32,2,8,2,48,128]{5,4,3,2,1,0:T(8,128)(2,1)} fusion(bf16[2,2,8,2,48,3,128]{6,4,5,3,2,1,0:T(8,128)(2,1)S(1)} %maximum_maximum_fusion, s32[32]{0:T(128)S(1)} %reshape.104), kind=kCustom, calls=%fused_computation | custom fusion | bytes 25166080 | tf_op jit(solution)/shard_map/gather | solution.py:70
  58.1 0.6 fusion.54
  58.7 0.1 fusion.33
  58.8 1.4 all-gather.2.cloned.1.call-done
  60.2 4.9 %fusion.9 = bf16[1,2,384,1536]{3,2,1,0:T(8,128)(2,1)S(1)} fusion(f32[]{:T(128)} %bitcast.18, bf16[8,2,128,1536]{3,2,0,1:T(8,128)(2,1)} %all-gather.2.cloned.1.call-done, s32[]{:T(128)S(6)} %select_n.36, bf16[1,8,2,48,384]{4,3,1,2,0:T(8,128)(2,1)} %get-tuple-element.11, bf16[1,8,2,48,384]{4,3,1,2,0:T(8,128)(2,1)} %bitcast.110), kind=kOutput, calls=%fused_computation.19 | convolution fusion | flops 1814888448 | bytes 5898756 | tf_op jit(solution)/shard_map/owpfr,wpfk->ork/dot_general | solution.py:50
  65.1 0.0 copy-done.5
  65.1 4.5 %fusion.8 = bf16[1,2,384,1536]{3,2,1,0:T(8,128)(2,1)S(1)} fusion(f32[]{:T(128)} %bitcast.8, bf16[8,2,128,1536]{3,2,0,1:T(8,128)(2,1)} %all-gather.2.cloned.1.call-done, s32[]{:T(128)S(6)} %select_n.35, bf16[1,8,2,48,384]{4,3,1,2,0:T(8,128)(2,1)S(1)} %copy-done.5, bf16[1,8,2,48,384]{4,3,1,2,0:T(8,128)(2,1)S(1)} %bitcast.109), kind=kOutput, calls=%fused_computation.18 | convolution fusion | flops 1814888448 | bytes 5898756 | tf_op jit(solution)/shard_map/owpfr,wpfk->ork/dot_general | solution.py:50
  69.7 2.6 %pad_maximum_fusion = bf16[2,2,384,1536]{3,2,1,0:T(8,128)(2,1)} fusion(bf16[1,2,384,1536]{3,2,1,0:T(8,128)(2,1)S(1)} %fusion.9, bf16[1,2,384,1536]{3,2,1,0:T(8,128)(2,1)S(1)} %fusion.8), kind=kLoop, calls=%fused_computation.10 | loop fusion | flops 2359296 | bytes 9437184 | tf_op jit(solution)/shard_map/stack | solution.py:52
  72.3 108.7 %all-to-all-done = bf16[8,4,8,2,48,128]{5,4,2,3,1,0:T(8,128)(2,1)} async-done(((bf16[8,4,8,2,48,128]{5,4,2,3,1,0:T(8,128)(2,1)}), bf16[8,4,8,2,48,128]{5,4,2,3,1,0:T(8,128)(2,1)}, u32[]{:S(2)}, u32[]{:S(2)}) %all-to-all-start) | async-done | bytes 6291488 | tf_op jit(solution)/shard_map/all_to_all | solution.py:67
  180.9 10.3 %fusion.18 = bf16[1,1,8,4,2,128,128]{6,5,4,3,2,1,0:T(8,128)(2,1)} fusion(f32[8,4]{1,0:T(8,128)S(1)} %fusion.33, bf16[8,4,8,2,48,128]{5,4,2,3,1,0:T(8,128)(2,1)} %all-to-all-done, bf16[8,4,2,8,2,48,128]{6,5,4,3,2,1,0:T(8,128)(2,1)} %bitcast.108), kind=kOutput, calls=%fused_computation.25 | convolution fusion | flops 1612709888 | bytes 20971648 | tf_op jit(solution)/shard_map/scowpfr,scwpfk->scork/dot_general | solution.py:71
  (11 shorter events, 0.0 us)
Async XLA Ops:
  7.2 8.6 %copy-start = (s32[1,8,8,4,3]{2,3,4,1,0:T(4,128)S(1)}, s32[1,8,8,4,3]{2,3,4,1,0:T(4,128)}, u32[]{:S(2)}) copy-start(s32[1,8,8,4,3]{2,3,4,1,0:T(4,128)} %param.6) | copy-start | bytes 9220
  7.2 2.3 %copy-start.3 = (bf16[8,2,128,384]{3,2,1,0:T(8,128)(2,1)S(1)}, bf16[8,2,128,384]{3,2,1,0:T(8,128)(2,1)}, u32[]{:S(2)}) copy-start(bf16[8,2,128,384]{3,2,1,0:T(8,128)(2,1)} %param.4) | copy-start | bytes 4718596
  7.2 53.0 %all-gather.2.cloned.1.call-start = ((), (), s32[]{:S(2)}) async-start(), calls=%async_computation.1 | async-start | bytes 7864320 | tf_op jit(solution)/shard_map/all_gather | solution.py:46
  9.5 1.6 copy-start.6
  9.5 4.7 %copy-start.7 = (s32[1,8,8]{2,1,0:T(8,128)S(1)}, s32[1,8,8]{2,1,0:T(8,128)}, u32[]{:S(2)}) copy-start(s32[1,8,8]{2,1,0:T(8,128)} %param.7) | copy-start | bytes 772
  11.0 6.4 %copy-start.2 = (bf16[8,2,128,384]{3,2,0,1:T(8,128)(2,1)S(1)}, bf16[8,2,128,384]{3,2,0,1:T(8,128)(2,1)}, u32[]{:S(2)}) copy-start(bf16[8,2,128,384]{3,2,0,1:T(8,128)(2,1)} %fusion.7) | copy-start | bytes 4718596
  19.0 27.2 %copy-start.4 = (bf16[8,2,48,384]{3,2,0,1:T(8,128)(2,1)}, bf16[8,2,48,384]{3,2,0,1:T(8,128)(2,1)S(1)}, u32[]{:S(2)}) copy-start(bf16[8,2,48,384]{3,2,0,1:T(8,128)(2,1)S(1)} %get-tuple-element.6) | copy-start | bytes 1769476
  35.3 145.6 %all-to-all-start = ((bf16[8,4,8,2,48,128]{5,4,2,3,1,0:T(8,128)(2,1)}), bf16[8,4,8,2,48,128]{5,4,2,3,1,0:T(8,128)(2,1)}, u32[]{:S(2)}, u32[]{:S(2)}) async-start(bf16[8,4,8,2,48,128]{5,4,2,3,1,0:T(8,128)(2,1)} %broadcast_multiply_fusion), calls=%async_computation | async-start | bytes 12582912 | tf_op jit(solution)/shard_map/all_to_all | solution.py:67
  60.2 4.9 %copy-start.5 = (bf16[1,8,2,48,384]{4,3,1,2,0:T(8,128)(2,1)S(1)}, bf16[1,8,2,48,384]{4,3,1,2,0:T(8,128)(2,1)}, u32[]{:S(2)}) copy-start(bf16[1,8,2,48,384]{4,3,1,2,0:T(8,128)(2,1)} %get-tuple-element.9) | copy-start | bytes 1769476
  180.9 10.3 %copy-start.1 = (s32[1,8,8,4,3]{2,3,4,1,0:T(4,128)S(1)}, s32[1,8,8,4,3]{2,3,4,1,0:T(4,128)}, u32[]{:S(2)}) copy-start(s32[1,8,8,4,3]{2,3,4,1,0:T(4,128)} %param.6) | copy-start | bytes 9220
Sparse Core Ops, SparseCore 0:
  11.2 48.9 all-gather.1
where the time goes:
time: 199 us; the launch traced here: 198 us
  waiting for transfers between devices  110 us (55%)
  local copies, waits for them, and re-layouts  25.2 us (13%)
  matrix products  20 us (10%)
  between operations  18 us (9%)
  other arithmetic  17.3 us (9%)
  starting transfers between devices  7.4 us (4%)
    all_to_all x1, waiting for transfers between devices, body(): lax.all_to_all(payload, 'seg', split_axis=0, concat_axis=0, tiled=True)  109 us
    dot_general x1, matrix products, body(): jnp.einsum('scowpfr,scwpfk->scork', chosen, arrived, preferred_element_ty...  10.3 us
    dot_general x2, matrix products, body(): jnp.einsum('owpfr,wpfk->ork', row_ops[band], cut, preferred_element_type=...  9.42 us
    gather x2, local copies, waits for them, and re-layouts, body(): blocks[sent[..., 2], :, :, :, sent[..., 1], :]  8.38 us
    all_to_all x1, starting transfers between devices, body(): lax.all_to_all(payload, 'seg', split_axis=0, concat_axis=0, tiled=True)  7.36 us
    gather x1, local copies, waits for them, and re-layouts, body(): chosen = op_blocks[taken[..., 2], :, :, :, :, taken[..., 0], :]  6.9 us
  transfers between devices with their start and end apart: 2, of which 2 were waited for; matrix products, arithmetic and copies ran while one was open for 24% of the time, Pallas kernels for 0%

commit v1 on v0

v1 whole, which is shorter than its diff:
```python
import functools

import jax
import jax.numpy as jnp
from jax import lax
from jax.experimental import pallas as pl
from jax.experimental.pallas import tpu as pltpu
from jax.sharding import PartitionSpec as P

W = 8
F = 128
BAND_MAX = 48
SMOOTH = 4
BLOCK = 128
BLK_DEV = 3
DEPTH = W * 2 * BAND_MAX
PIECES = 2 * BLK_DEV
LINE_Z = 4
CORES = 2


HIGH = lax.Precision.HIGHEST
MESH = pl.DeviceIdType.MESH


def whiten_gain(spectra):
    values = spectra.astype(jnp.float32)
    power = jnp.sum(values * values, axis=(0, 1))
    bins = jnp.arange(F)
    window = (jnp.abs(bins[:, None] - bins[None, :]) <= SMOOTH).astype(jnp.float32)
    totals = jnp.sum(window, axis=1) * W
    level = (
        jnp.dot(window, power, precision=HIGH, preferred_element_type=jnp.float32) / totals[:, None]
    )
    return lax.rsqrt(level + 1e-06)


def band_operands(spectra, gain, band_bins):
    cols = []
    ops = []
    for band in range(2):
        start = band_bins[band, 0]
        values = lax.dynamic_slice_in_dim(spectra, start, BAND_MAX, 2).astype(jnp.float32)
        scale = lax.dynamic_slice_in_dim(gain, start, BAND_MAX, 0)
        piece = (values * scale[None, None]).astype(jnp.bfloat16)
        piece = piece.reshape(W, 2, BAND_MAX, BLK_DEV, BLOCK)
        live = (jnp.arange(BAND_MAX) < band_bins[band, 1]).astype(jnp.bfloat16)
        rows = piece * live[None, None, :, None, None]
        twisted = jnp.stack([rows[:, 1], -rows[:, 0]], axis=1)
        cols.append(jnp.transpose(piece.reshape(DEPTH, BLK_DEV, BLOCK), (1, 0, 2)))
        both = jnp.stack([rows, twisted], axis=0).reshape(2, DEPTH, BLK_DEV, BLOCK)
        ops.append(jnp.transpose(both, (2, 0, 3, 1)).reshape(BLK_DEV, 2 * BLOCK, DEPTH))
    scales = lax.rsqrt((W * band_bins[:, 1]).astype(jnp.float32))
    return (jnp.concatenate(cols), jnp.stack(ops), scales)


class Gather:
    def __init__(self, axis, high, low, own, buf, send, recv):
        self.axis, self.high, self.low = axis, high, low
        self.own, self.buf, self.send, self.recv = own, buf, send, recv
        self.me = lax.axis_index(axis)
        self.p, self.l = lax.div(self.me, low), lax.rem(self.me, low)
        p, l = self.p, self.l
        self.dirs = [
            (p + 1 < high, self.me + low),
            (p > 0, self.me - low),
            (l + 1 < low, self.me + 1),
            (l > 0, self.me - 1),
        ]
        if high == 1:
            self.dirs[0] = self.dirs[1] = None
        if low == 1:
            self.dirs[2] = self.dirs[3] = None
        self.closing = False

    def greet(self, barrier):
        for entry in self.dirs:
            if entry is not None:

                @pl.when(entry[0])
                def _():
                    pl.semaphore_signal(
                        barrier, inc=1, device_id={self.axis: entry[1]}, device_id_type=MESH
                    )

    def peers(self):
        return sum(jnp.where(entry[0], 1, 0) for entry in self.dirs if entry is not None)

    def copy(self, way, src, q, own):
        return pltpu.make_async_remote_copy(
            src_ref=self.own.at[q] if own else self.buf.at[src, q],
            dst_ref=self.buf.at[src, q],
            send_sem=self.send.at[way, src, q],
            recv_sem=self.recv.at[src, q],
            device_id={self.axis: self.dirs[way][1]},
            device_id_type=MESH,
        )

    def pass_on(self, ways, src, q, own=False):
        for way in ways:
            if self.dirs[way] is not None:

                @pl.when(self.dirs[way][0])
                def _():
                    piece = self.copy(way, src, q, own)
                    if self.closing:
                        piece.wait_send()
                    else:
                        piece.start()

    def arrive(self, there, src, q, ways, use):
        @pl.when(there)
        def _():
            if not self.closing:
                pltpu.make_async_copy(
                    self.buf.at[src, q], self.buf.at[src, q], self.recv.at[src, q]
                ).wait()
            self.pass_on(ways, src, q)
            if use is not None and not self.closing:
                use(src, q)

    def start(self, q):
        self.pass_on((0, 1, 2, 3), self.me, q, own=True)

    def step(self, st, q, use):
        p, l, low = self.p, self.l, self.low
        if 0 < st < self.high:
            self.arrive(p - st >= 0, (p - st) * low + l, q, (0, 2, 3), use)
            self.arrive(p + st < self.high, (p + st) * low + l, q, (1, 2, 3), use)
        d = st - 1
        if 0 <= d < self.high:
            for far in [p] if d == 0 else [p - d, p + d]:
                inside = (far >= 0) & (far < self.high)
                for e in range(1, low):
                    self.arrive(inside & (l - e >= 0), far * low + l - e, q, (2,), use)
                    self.arrive(inside & (l + e < low), far * low + l + e, q, (3,), use)


def kernel(
    nseg, ngrp, lists, factors, scales, cols, ops, near, far, seg_buf, grp_buf,
    seg_send, seg_recv, grp_send, grp_recv, move,
):
    seg = Gather("seg", LINE_Z, nseg // LINE_Z, cols, seg_buf, seg_send, seg_recv)
    grp = Gather("grp", ngrp // CORES, CORES, cols, grp_buf, grp_send, grp_recv)
    barrier = pltpu.get_barrier_semaphore()
    seg.greet(barrier)
    grp.greet(barrier)
    pl.semaphore_wait(barrier, seg.peers() + grp.peers())

    def loop(fn):
        def step(q, carry):
            fn(q)
            return carry

        lax.fori_loop(0, PIECES, step, 0)

    def near_from(piece, src, q):
        band, m = lax.div(q, BLK_DEV), lax.rem(q, BLK_DEV)
        at = pl.ds(pl.multiple_of(src * (BLK_DEV * BLOCK) + m * BLOCK, BLOCK), BLOCK)
        for i in range(BLK_DEV):
            prod = jnp.dot(ops[band, i], piece, preferred_element_type=jnp.float32)
            prod = (prod * scales[band]).astype(jnp.bfloat16)
            near[band, 0, i * BLOCK : (i + 1) * BLOCK, at] = prod[:BLOCK]
            near[band, 1, i * BLOCK : (i + 1) * BLOCK, at] = prod[BLOCK:]

    def use_near(src, q):
        near_from(grp_buf[src, q], src, q)

    def begin(q):
        seg.start(q)
        grp.start(q)

    loop(begin)
    loop(lambda q: near_from(cols[q], grp.me, q))

    def steps():
        for st in range(1, max(seg.high, grp.high) + 1):

            def both(q):
                seg.step(st, q, None)
                grp.step(st, q, use_near)

            loop(both)

    steps()

    own = pltpu.make_async_copy(cols, seg_buf.at[seg.me], move)
    own.start()
    own.wait()

    def far_source(t, carry):
        for c in range(lists.shape[1] // 3):
            i, m, band = lists[t, 3 * c], lists[t, 3 * c + 1], lists[t, 3 * c + 2]
            prod = jnp.dot(
                ops[band, i], seg_buf[t, band * BLK_DEV + m], preferred_element_type=jnp.float32
            )
            prod = (prod * factors[t, c]).astype(jnp.bfloat16)
            far[t, c, 0] = prod[:BLOCK]
            far[t, c, 1] = prod[BLOCK:]
        return carry

    lax.fori_loop(0, nseg, far_source, 0)

    seg.closing = grp.closing = True
    loop(begin)
    steps()


def body(nseg, ngrp, spectra, band_bins, far_list, far_count):
    gain = whiten_gain(spectra)
    cols, ops, scales = band_operands(spectra, gain, band_bins)
    seg_index = lax.axis_index("seg")
    taken = lax.dynamic_index_in_dim(far_list[0], seg_index, 0, keepdims=False)
    count = lax.dynamic_index_in_dim(far_count[0], seg_index, 0, keepdims=False)
    slots = taken.shape[1]
    live = (jnp.arange(slots)[None, :] < count[:, None]).astype(jnp.float32)
    factors = scales[taken[..., 2]] * live
    smem = pl.BlockSpec(memory_space=pltpu.SMEM)
    vmem = pl.BlockSpec(memory_space=pltpu.VMEM)
    sems = pltpu.SemaphoreType.DMA
    near, far = pl.pallas_call(
        functools.partial(kernel, nseg, ngrp),
        out_shape=(
            jax.ShapeDtypeStruct(
                (2, 2, BLK_DEV * BLOCK, ngrp * BLK_DEV * BLOCK), jnp.bfloat16
            ),
            jax.ShapeDtypeStruct((nseg, slots, 2, BLOCK, BLOCK), jnp.bfloat16),
        ),
        in_specs=[smem, smem, smem, vmem, vmem],
        out_specs=(vmem, vmem),
        scratch_shapes=[
            pltpu.VMEM((nseg, PIECES, DEPTH, BLOCK), jnp.bfloat16),
            pltpu.VMEM((ngrp, PIECES, DEPTH, BLOCK), jnp.bfloat16),
            sems((4, nseg, PIECES)),
            sems((nseg, PIECES)),
            sems((4, ngrp, PIECES)),
            sems((ngrp, PIECES)),
            sems,
        ],
        compiler_params=pltpu.CompilerParams(
            collective_id=0, has_side_effects=True, vmem_limit_bytes=56 * 1024 * 1024
        ),
    )(taken.reshape(nseg, slots * 3), factors, scales, cols, ops)
    return (near, far[None, None])


def solution(mesh):
    placed = (
        P(None, None, None, ("seg", "grp")),
        P(),
        P("grp", None, None, None, None),
        P("grp", None, None),
    )
    return jax.shard_map(
        functools.partial(body, mesh.shape["seg"], mesh.shape["grp"]),
        mesh=mesh,
        in_specs=placed,
        out_specs=(
            P(None, None, ("seg", "grp"), None),
            P("seg", "grp", None, None, None, None, None),
        ),
        check_vma=False,
    )
```

time: 199 us -> 162 us (0.81)
  Pallas kernels: 0 us -> 120 us
  waiting for transfers between devices: 110 us -> 0 us
  matrix products: 20 us -> 0.27 us
  between operations: 18 us -> 4.52 us
  local copies, waits for them, and re-layouts: 25.2 us -> 17.7 us
  starting transfers between devices: 7.4 us -> 0 us
    pallas_call x0 -> x1, Pallas kernels: none -> 120 us  [body(): pl.pallas_call(functools.partial(kernel, nseg, ngrp), out_shape=(jax.Shap...]
    all_to_all x1 -> x0, waiting for transfers between devices: 109 us -> none  [body(): lax.all_to_all(payload, 'seg', split_axis=0, concat_axis=0, tiled=True)]
    dot_general x4 -> x1, matrix products: 20 us -> 0.27 us  [whiten_gain(): jnp.dot(window, power, precision=HIGH, preferred_element_type=jnp.float32)]
    gather x5 -> x2, local copies, waits for them, and re-layouts: 16.1 us -> 0.77 us  [body(): factors = scales[taken[..., 2]] * live]
    all_to_all x1 -> x0, starting transfers between devices: 7.36 us -> none  [body(): lax.all_to_all(payload, 'seg', split_axis=0, concat_axis=0, tiled=True)]
    unnamed x16, local copies, waits for them, and re-layouts: 0.05 us -> 7.27 us
    another operation x12 -> x2, local copies, waits for them, and re-layouts: 6.99 us -> 1.17 us  [band_operands(): cols.append(jnp.transpose(piece.reshape(DEPTH, BLK_DEV, BLOCK), (1, 0, 2)))]
    transpose x0 -> x3, local copies, waits for them, and re-layouts: none -> 4.32 us  [the longest x2 4.15 us: band_operands(): jnp.transpose(both, (2, 0, 3, 1)).reshape(BLK_DEV, 2 * BLOCK, DEPTH)]
  transfers between devices with their start and end apart: 2 -> 0, of which waited for: 2 -> 0; matrix products, arithmetic and copies ran while one was open for 24% -> 0% of each run, Pallas kernels for 0% -> 0%
where the time goes in v1:
time: 162 us
  Pallas kernels  120 us (74%)
  other arithmetic  19.1 us (12%)
  local copies, waits for them, and re-layouts  17.7 us (11%)
  between operations  4.52 us (3%)
    pallas_call x1, Pallas kernels, body(): pl.pallas_call(functools.partial(kernel, nseg, ngrp), out_shape=(jax.Shap...  120 us
    unnamed x16, local copies, waits for them, and re-layouts  7.27 us
    mul x4, other arithmetic, band_operands(): rows = piece * live[None, None, :, None, None]  6.45 us
    transpose x2, local copies, waits for them, and re-layouts, band_operands(): jnp.transpose(both, (2, 0, 3, 1)).reshape(BLK_DEV, 2 * BLOCK, DEPTH)  4.15 us

profile of v1, /device:TPU:0, one launch (start us, length us, event | category | flops | bytes accessed | tf_op | source)
XLA Modules:
  0.0 162.0 jit_solution(821927027668600525)
XLA Ops:
  0.6 0.0 copy-start
  0.6 0.9 rsqrt_reduce_fusion.scales
  1.5 0.0 copy-start.1
  1.5 0.7 fusion.4
  2.2 0.1 convert_reduce_fusion
  2.4 1.5 fusion.8
  7.5 0.7 compare_convert_fusion.1
  8.1 0.7 compare_convert_fusion
  8.8 0.1 mul.100
  8.9 0.1 mul.94
  9.0 0.0 copy-done
  9.1 0.1 copy.25
  9.1 0.1 reshape.82
  9.2 0.0 copy-start.2
  9.3 0.7 gather_fusion
  9.9 0.0 copy-done.1
  10.0 0.1 reshape.81
  10.0 0.7 fusion.3.factors
  10.7 0.1 copy.35
  10.8 0.7 reshape.89.lists
  11.5 0.0 copy-done.2
  11.5 0.3 multiply_reduce_fusion
  11.8 0.3 fusion.1
  12.1 0.6 multiply_convert_fusion.1
  12.7 0.2 reshape.77
  12.9 0.4 broadcast_multiply_fusion.1
  13.3 0.3 fusion.6
  13.6 1.4 pad_maximum_fusion.2
  15.0 0.2 reshape.76
  15.2 0.0 copy-start.4
  15.2 2.8 %broadcast_multiply_fusion.3 = bf16[1,768,3,128]{3,2,1,0:T(4,128)(2,1)S(1)} fusion(bf16[1,768,3,128]{3,2,1,0:T(4,128)(2,1)S(1)} %reshape.76, bf16[768]{0:T(1024)(128)(2,1)S(1)} %mul.94), kind=kLoop, calls=%fused_computation.18 | loop fusion | flops 294912 | bytes 1181184 | tf_op jit(solution)/shard_map/mul | solution.py:48
  18.0 0.0 copy-done.4
  18.1 1.1 maximum_bitcast_fusion
  19.2 2.1 %copy.30 = bf16[3,2,128,768]{3,2,1,0:T(8,128)(2,1)} copy(bf16[3,2,128,768]{2,0,3,1:T(4,128)(2,1)S(1)} %maximum_bitcast_fusion) | data formatting | bytes 2359296 | tf_op jit(solution)/shard_map/transpose | solution.py:52
  21.3 1.0 reshape_reshape.6
  22.2 0.2 reshape.79
  22.4 0.4 broadcast_multiply_fusion
  22.9 0.3 fusion.7
  23.2 0.5 pad_maximum_fusion.3
  23.7 0.2 reshape.78
  23.9 2.8 %broadcast_multiply_fusion.2 = bf16[1,768,3,128]{3,2,1,0:T(4,128)(2,1)S(1)} fusion(bf16[1,768,3,128]{3,2,1,0:T(4,128)(2,1)S(1)} %reshape.78, bf16[768]{0:T(1024)(128)(2,1)S(1)} %mul.100), kind=kLoop, calls=%fused_computation.17 | loop fusion | flops 294912 | bytes 1181184 | tf_op jit(solution)/shard_map/mul | solution.py:48
  26.7 1.1 maximum_bitcast_fusion.1
  27.8 0.0 copy-start.3
  27.8 2.1 %copy.33 = bf16[3,2,128,768]{3,2,1,0:T(8,128)(2,1)} copy(bf16[3,2,128,768]{2,0,3,1:T(4,128)(2,1)S(1)} %maximum_bitcast_fusion.1) | data formatting | bytes 2359296 | tf_op jit(solution)/shard_map/transpose | solution.py:52
  29.9 0.0 copy-done.3
  29.9 2.9 %pad_maximum_fusion.ops = bf16[2,3,256,768]{3,2,1,0:T(8,128)(2,1)} fusion(bf16[1,3,256,768]{3,2,1,0:T(8,128)(2,1)} %bitcast.37, bf16[1,3,256,768]{3,2,1,0:T(8,128)(2,1)S(1)} %bitcast.36), kind=kLoop, calls=%fused_computation.2 | loop fusion | flops 1179648 | bytes 4718592 | tf_op jit(solution)/shard_map/stack | solution.py:54
  32.8 0.0 copy-start.5
  32.8 0.2 reshape_reshape.7
  33.0 0.9 copy-done.5
  33.9 0.2 copy_bitcast_fusion
  34.1 1.1 pad_maximum_fusion.1.cols
  35.2 120.4 %shard_map.59 = (bf16[2,2,384,1536]{3,2,1,0:T(8,128)(2,1)}, bf16[8,4,2,128,128]{4,3,2,1,0:T(8,128)(2,1)}) custom-call(s32[8,12]{1,0:T(8,128)} %reshape.89.lists, f32[8,4]{1,0:T(8,128)} %fusion.3.factors, f32[2]{0:T(128)} %copy-done.1, bf16[6,768,128]{2,1,0:T(8,128)(2,1)} %pad_maximum_fusion.1.cols, bf16[2,3,256,768]{3,2,1,0:T(8,128)(2,1)} %pad_maximum_fusion.ops), custom_call_target="tpu_custom_call" | custom-call | tf_op jit(solution)/shard_map/pallas_call | solution.py:221
  155.7 0.0 copy-start.6
  155.7 5.0 %copy.43 = bf16[2,2,384,1536]{3,2,1,0:T(8,128)(2,1)} copy(bf16[2,2,384,1536]{3,2,1,0:T(8,128)(2,1)} %get-tuple-element.22) | data formatting | bytes 9437184
  160.7 0.0 copy-done.6
  160.7 1.3 copy.44
  (8 shorter events, 0.1 us)
Async XLA Ops:
  0.6 8.4 %copy-start = (s32[1,8,8,4,3]{2,3,4,1,0:T(4,128)S(1)}, s32[1,8,8,4,3]{2,3,4,1,0:T(4,128)}, u32[]{:S(2)}) copy-start(s32[1,8,8,4,3]{2,3,4,1,0:T(4,128)} %param.6) | copy-start | bytes 9220
  1.5 8.4 %copy-start.1 = (f32[2]{0:T(128)}, f32[2]{0:T(128)S(1)}, u32[]{:S(2)}) copy-start(f32[2]{0:T(128)S(1)} %rsqrt_reduce_fusion.scales) | copy-start | bytes 28
  9.2 2.2 %copy-start.2 = (bf16[8,2,128,384]{3,2,1,0:T(8,128)(2,1)S(1)}, bf16[8,2,128,384]{3,2,1,0:T(8,128)(2,1)}, u32[]{:S(2)}) copy-start(bf16[8,2,128,384]{3,2,1,0:T(8,128)(2,1)} %param.4) | copy-start | bytes 4718596
  15.2 2.8 %copy-start.4 = (bf16[8,2,48,3,128]{4,3,2,1,0:T(4,128)(2,1)S(1)}, bf16[8,2,48,3,128]{4,3,2,1,0:T(4,128)(2,1)}, u32[]{:S(2)}) copy-start(bf16[8,2,48,3,128]{4,3,2,1,0:T(4,128)(2,1)} %pad_maximum_fusion.2) | copy-start | bytes 1769476
  27.8 2.1 %copy-start.3 = (bf16[3,2,128,768]{3,2,1,0:T(8,128)(2,1)S(1)}, bf16[3,2,128,768]{3,2,1,0:T(8,128)(2,1)}, u32[]{:S(2)}) copy-start(bf16[3,2,128,768]{3,2,1,0:T(8,128)(2,1)} %copy.30) | copy-start | bytes 3538948
  32.8 1.1 copy-start.5
  155.7 5.0 %copy-start.6 = (bf16[8,4,2,128,128]{4,3,2,1,0:T(8,128)(2,1)S(1)}, bf16[8,4,2,128,128]{4,3,2,1,0:T(8,128)(2,1)}, u32[]{:S(2)}) copy-start(bf16[8,4,2,128,128]{4,3,2,1,0:T(8,128)(2,1)} %get-tuple-element.5) | copy-start | bytes 6291460

commit v2 on v1

--- a/solution.py
+++ b/solution.py
@@ -23,35 +23,41 @@
 MESH = pl.DeviceIdType.MESH
 
 
-def whiten_gain(spectra):
-    values = spectra.astype(jnp.float32)
-    power = jnp.sum(values * values, axis=(0, 1))
-    bins = jnp.arange(F)
-    window = (jnp.abs(bins[:, None] - bins[None, :]) <= SMOOTH).astype(jnp.float32)
-    totals = jnp.sum(window, axis=1) * W
-    level = (
-        jnp.dot(window, power, precision=HIGH, preferred_element_type=jnp.float32) / totals[:, None]
-    )
-    return lax.rsqrt(level + 1e-06)
-
-
-def band_operands(spectra, gain, band_bins):
-    cols = []
-    ops = []
+def whiten_kernel(bins, spectra, cols, gain):
+    power = jnp.zeros((F, BLOCK), jnp.float32)
+    for w in range(W):
+        for p in range(2):
+            values = spectra[w, p].astype(jnp.float32)
+            power = power + values * values
+    f = lax.broadcasted_iota(jnp.int32, (F, F), 0)
+    g = lax.broadcasted_iota(jnp.int32, (F, F), 1)
+    window = jnp.where(jnp.abs(f - g) <= SMOOTH, 1.0, 0.0).astype(jnp.float32)
+    totals = jnp.sum(window, axis=1, keepdims=True) * W
+    level = jnp.dot(window, power, precision=HIGH, preferred_element_type=jnp.float32) / totals
+    gain[...] = lax.rsqrt(level + 1e-06)
     for band in range(2):
-        start = band_bins[band, 0]
-        values = lax.dynamic_slice_in_dim(spectra, start, BAND_MAX, 2).astype(jnp.float32)
-        scale = lax.dynamic_slice_in_dim(gain, start, BAND_MAX, 0)
-        piece = (values * scale[None, None]).astype(jnp.bfloat16)
-        piece = piece.reshape(W, 2, BAND_MAX, BLK_DEV, BLOCK)
-        live = (jnp.arange(BAND_MAX) < band_bins[band, 1]).astype(jnp.bfloat16)
-        rows = piece * live[None, None, :, None, None]
-        twisted = jnp.stack([rows[:, 1], -rows[:, 0]], axis=1)
-        cols.append(jnp.transpose(piece.reshape(DEPTH, BLK_DEV, BLOCK), (1, 0, 2)))
-        both = jnp.stack([rows, twisted], axis=0).reshape(2, DEPTH, BLK_DEV, BLOCK)
-        ops.append(jnp.transpose(both, (2, 0, 3, 1)).reshape(BLK_DEV, 2 * BLOCK, DEPTH))
-    scales = lax.rsqrt((W * band_bins[:, 1]).astype(jnp.float32))
-    return (jnp.concatenate(cols), jnp.stack(ops), scales)
+        at = pl.ds(pl.multiple_of(bins[band, 0], 16), BAND_MAX)
+        scale = gain[at]
+        for p in range(2):
+            for w in range(W):
+                first = (p * W + w) * BAND_MAX
+                piece = spectra[w, p, at].astype(jnp.float32) * scale
+                cols[band, 0, first : first + BAND_MAX] = piece.astype(jnp.bfloat16)
+
+
+def band_columns(spectra, band_bins):
+    return pl.pallas_call(
+        whiten_kernel,
+        grid=(BLK_DEV,),
+        out_shape=jax.ShapeDtypeStruct((2, BLK_DEV, DEPTH, BLOCK), jnp.bfloat16),
+        in_specs=[
+            pl.BlockSpec(memory_space=pltpu.SMEM),
+            pl.BlockSpec((W, 2, F, BLOCK), lambda m: (0, 0, 0, m)),
+        ],
+        out_specs=pl.BlockSpec((2, 1, DEPTH, BLOCK), lambda m: (0, m, 0, 0)),
+        scratch_shapes=[pltpu.VMEM((F, BLOCK), jnp.float32)],
+        compiler_params=pltpu.CompilerParams(vmem_limit_bytes=56 * 1024 * 1024),
+    )(band_bins, spectra).reshape(PIECES, DEPTH, BLOCK)
 
 
 class Gather:
@@ -122,22 +128,30 @@
     def start(self, q):
         self.pass_on((0, 1, 2, 3), self.me, q, own=True)
 
-    def step(self, st, q, use):
+    def step(self, st, q, use, low_first=False):
         p, l, low = self.p, self.l, self.low
+        turn = () if low_first else (2, 3)
         if 0 < st < self.high:
-            self.arrive(p - st >= 0, (p - st) * low + l, q, (0, 2, 3), use)
-            self.arrive(p + st < self.high, (p + st) * low + l, q, (1, 2, 3), use)
+            self.arrive(p - st >= 0, (p - st) * low + l, q, (0,) + turn, use)
+            self.arrive(p + st < self.high, (p + st) * low + l, q, (1,) + turn, use)
         d = st - 1
-        if 0 <= d < self.high:
-            for far in [p] if d == 0 else [p - d, p + d]:
-                inside = (far >= 0) & (far < self.high)
-                for e in range(1, low):
-                    self.arrive(inside & (l - e >= 0), far * low + l - e, q, (2,), use)
-                    self.arrive(inside & (l + e < low), far * low + l + e, q, (3,), use)
+        if not 0 <= d < self.high:
+            return
+        for far, way in [(p, None)] if d == 0 else [(p - d, 0), (p + d, 1)]:
+            inside = (far >= 0) & (far < self.high)
+            for e in range(1, low):
+                for there, other, on in ((l - e >= 0, l - e, 2), (l + e < low, l + e, 3)):
+                    if not low_first:
+                        ways = (on,)
+                    elif d == 0:
+                        ways = (0, 1, on)
+                    else:
+                        ways = (way,)
+                    self.arrive(inside & there, far * low + other, q, ways, use)
 
 
 def kernel(
-    nseg, ngrp, lists, factors, scales, cols, ops, near, far, seg_buf, grp_buf,
+    nseg, ngrp, bins, lists, counts, cols, near, far, seg_buf, grp_buf, ops,
     seg_send, seg_recv, grp_send, grp_recv, move,
 ):
     seg = Gather("seg", LINE_Z, nseg // LINE_Z, cols, seg_buf, seg_send, seg_recv)
@@ -147,54 +161,77 @@
     grp.greet(barrier)
     pl.semaphore_wait(barrier, seg.peers() + grp.peers())
 
-    def loop(fn):
+    def loop(fn, first=0):
         def step(q, carry):
             fn(q)
             return carry
 
-        lax.fori_loop(0, PIECES, step, 0)
+        lax.fori_loop(first, PIECES, step, 0)
+
+    def begin(q):
+        seg.start(q)
+        grp.start(q)
+
+    loop(begin)
+    own = pltpu.make_async_copy(cols, seg_buf.at[seg.me], move)
+    own.start()
+
+    half = DEPTH // 2
+
+    def operands(q):
+        band, m = lax.div(q, BLK_DEV), lax.rem(q, BLK_DEV)
+        bin_of = lax.rem(lax.broadcasted_iota(jnp.int32, (1, DEPTH), 1), BAND_MAX)
+        live = jnp.where(bin_of < bins[band, 1], 1.0, 0.0).astype(jnp.float32)
+        rows = jnp.transpose(cols[q].astype(jnp.float32)) * live
+        ops[band, m, :BLOCK] = rows.astype(jnp.bfloat16)
+        ops[band, m, BLOCK:, :half] = rows[:, half:].astype(jnp.bfloat16)
+        ops[band, m, BLOCK:, half:] = (-rows[:, :half]).astype(jnp.bfloat16)
+
+    loop(operands)
+
+    def scale(band):
+        return lax.rsqrt(jnp.full((1, BLOCK), W * bins[band, 1], jnp.int32).astype(jnp.float32))
 
     def near_from(piece, src, q):
         band, m = lax.div(q, BLK_DEV), lax.rem(q, BLK_DEV)
         at = pl.ds(pl.multiple_of(src * (BLK_DEV * BLOCK) + m * BLOCK, BLOCK), BLOCK)
         for i in range(BLK_DEV):
             prod = jnp.dot(ops[band, i], piece, preferred_element_type=jnp.float32)
-            prod = (prod * scales[band]).astype(jnp.bfloat16)
+            prod = (prod * scale(band)).astype(jnp.bfloat16)
             near[band, 0, i * BLOCK : (i + 1) * BLOCK, at] = prod[:BLOCK]
             near[band, 1, i * BLOCK : (i + 1) * BLOCK, at] = prod[BLOCK:]
 
     def use_near(src, q):
         near_from(grp_buf[src, q], src, q)
 
-    def begin(q):
-        seg.start(q)
-        grp.start(q)
-
-    loop(begin)
     loop(lambda q: near_from(cols[q], grp.me, q))
 
     def steps():
         for st in range(1, max(seg.high, grp.high) + 1):
 
-            def both(q):
-                seg.step(st, q, None)
+            def both(q, low_first=False):
+                seg.step(st, q, None, low_first)
                 grp.step(st, q, use_near)
 
-            loop(both)
+            both(jnp.int32(0), low_first=True)
+            loop(both, 1)
 
     steps()
-
-    own = pltpu.make_async_copy(cols, seg_buf.at[seg.me], move)
-    own.start()
     own.wait()
 
+    slots = far.shape[1]
+
     def far_source(t, carry):
-        for c in range(lists.shape[1] // 3):
-            i, m, band = lists[t, 3 * c], lists[t, 3 * c + 1], lists[t, 3 * c + 2]
+        for c in range(slots):
+            entry = (t * slots + c) * 3
+            i = lists[seg.me, entry]
+            m = lists[seg.me, entry + 1]
+            band = lists[seg.me, entry + 2]
+            factor = jnp.where(c < counts[seg.me, t], scale(band), 0.0)
             prod = jnp.dot(
                 ops[band, i], seg_buf[t, band * BLK_DEV + m], preferred_element_type=jnp.float32
             )
-            prod = (prod * factors[t, c]).astype(jnp.bfloat16)
+            prod = (prod * factor).astype(jnp.bfloat16)
             far[t, c, 0] = prod[:BLOCK]
             far[t, c, 1] = prod[BLOCK:]
         return carry
@@ -207,14 +244,8 @@
 
 
 def body(nseg, ngrp, spectra, band_bins, far_list, far_count):
-    gain = whiten_gain(spectra)
-    cols, ops, scales = band_operands(spectra, gain, band_bins)
-    seg_index = lax.axis_index("seg")
-    taken = lax.dynamic_index_in_dim(far_list[0], seg_index, 0, keepdims=False)
-    count = lax.dynamic_index_in_dim(far_count[0], seg_index, 0, keepdims=False)
-    slots = taken.shape[1]
-    live = (jnp.arange(slots)[None, :] < count[:, None]).astype(jnp.float32)
-    factors = scales[taken[..., 2]] * live
+    cols = band_columns(spectra, band_bins)
+    slots = far_list.shape[3]
     smem = pl.BlockSpec(memory_space=pltpu.SMEM)
     vmem = pl.BlockSpec(memory_space=pltpu.VMEM)
     sems = pltpu.SemaphoreType.DMA
@@ -226,11 +257,12 @@
             ),
             jax.ShapeDtypeStruct((nseg, slots, 2, BLOCK, BLOCK), jnp.bfloat16),
         ),
-        in_specs=[smem, smem, smem, vmem, vmem],
+        in_specs=[smem, smem, smem, vmem],
         out_specs=(vmem, vmem),
         scratch_shapes=[
             pltpu.VMEM((nseg, PIECES, DEPTH, BLOCK), jnp.bfloat16),
             pltpu.VMEM((ngrp, PIECES, DEPTH, BLOCK), jnp.bfloat16),
+            pltpu.VMEM((2, BLK_DEV, 2 * BLOCK, DEPTH), jnp.bfloat16),
             sems((4, nseg, PIECES)),
             sems((nseg, PIECES)),
             sems((4, ngrp, PIECES)),
@@ -240,7 +272,7 @@
         compiler_params=pltpu.CompilerParams(
             collective_id=0, has_side_effects=True, vmem_limit_bytes=56 * 1024 * 1024
         ),
-    )(taken.reshape(nseg, slots * 3), factors, scales, cols, ops)
+    )(band_bins, far_list.reshape(nseg, nseg * slots * 3), far_count[0], cols)
     return (near, far[None, None])
 
 

time: 162 us -> 121 us (0.75)
  other arithmetic: 19.1 us -> 0 us
  local copies, waits for them, and re-layouts: 17.7 us -> 7.88 us
  Pallas kernels: 120 us -> 112 us
  between operations: 4.52 us -> 0.66 us
    pallas_call x1, Pallas kernels: 120 us -> 109 us  [body(): pl.pallas_call(functools.partial(kernel, nseg, ngrp), out_shape=(jax.Shap...]
    mul x6 -> x0, other arithmetic: 7.12 us -> none  [the longest x4 6.45 us: band_operands(): rows = piece * live[None, None, :, None, None]]
    another operation x3 -> x0, other arithmetic: 4.79 us -> none  [the longest x1 2.89 us: band_operands(): return (jnp.concatenate(cols), jnp.stack(ops), scales)]
    transpose x3 -> x0, local copies, waits for them, and re-layouts: 4.32 us -> none  [the longest x2 4.15 us: band_operands(): jnp.transpose(both, (2, 0, 3, 1)).reshape(BLK_DEV, 2 * BLOCK, DEPTH)]
    pallas_call x0 -> x1, Pallas kernels: none -> 3.69 us  [band_columns(): pl.pallas_call(whiten_kernel, grid=(BLK_DEV,), out_shape=jax.ShapeDtypeSt...]
    transpose x2 -> x0, other arithmetic: 2.22 us -> none  [band_operands(): jnp.transpose(both, (2, 0, 3, 1)).reshape(BLK_DEV, 2 * BLOCK, DEPTH)]
    convert_element_type x3 -> x0, other arithmetic: 1.92 us -> none  [the longest x2 1.34 us: band_operands(): live = (jnp.arange(BAND_MAX) < band_bins[band, 1]).astype(jnp.bfloat16)]
    unnamed x16 -> x5, local copies, waits for them, and re-layouts: 7.27 us -> 7.2 us
where the time goes in v2:
time: 121 us
  Pallas kernels  112 us (93%)
  local copies, waits for them, and re-layouts  7.88 us (7%)
    pallas_call x1, Pallas kernels, body(): pl.pallas_call(functools.partial(kernel, nseg, ngrp), out_shape=(jax.Shap...  109 us
    unnamed x5, local copies, waits for them, and re-layouts  7.2 us
    pallas_call x1, Pallas kernels, band_columns(): pl.pallas_call(whiten_kernel, grid=(BLK_DEV,), out_shape=jax.ShapeDtypeSt...  3.69 us

profile of v2, /device:TPU:0, one launch (start us, length us, event | category | flops | bytes accessed | tf_op | source)
XLA Modules:
  0.0 121.0 jit_solution(7390662123326876957)
XLA Ops:
  0.6 0.9 copy.7
  1.6 0.7 copy.8.lists
  2.2 3.7 %shard_map.59 = bf16[2,3,768,128]{3,2,1,0:T(8,128)(2,1)} custom-call(s32[2,2]{1,0:T(2,128)} %bins.3, bf16[8,2,128,384]{3,2,1,0:T(8,128)(2,1)} %spectra.1), custom_call_target="tpu_custom_call" | custom-call | tf_op jit(solution)/shard_map/pallas_call | solution.py:49
  5.9 108.8 %shard_map.60 = (bf16[2,2,384,1536]{3,2,1,0:T(8,128)(2,1)}, bf16[8,4,2,128,128]{4,3,2,1,0:T(8,128)(2,1)}) custom-call(s32[2,2]{1,0:T(2,128)} %bins.3, s32[8,96]{1,0:T(8,128)} %copy.8.lists, s32[8,8]{1,0:T(8,128)} %bitcast.7, bf16[6,768,128]{2,1,0:T(8,128)(2,1)} %bitcast.5), custom_call_target="tpu_custom_call" | custom-call | tf_op jit(solution)/shard_map/pallas_call | solution.py:252
  114.7 0.0 copy-start
  114.7 5.0 %copy.11 = bf16[2,2,384,1536]{3,2,1,0:T(8,128)(2,1)} copy(bf16[2,2,384,1536]{3,2,1,0:T(8,128)(2,1)} %get-tuple-element.8) | data formatting | bytes 9437184
  119.7 0.0 copy-done
  119.7 1.3 %copy.12 = bf16[1,1,8,4,2,128,128]{6,5,4,3,2,1,0:T(8,128)(2,1)} copy(bf16[1,1,8,4,2,128,128]{6,5,4,3,2,1,0:T(8,128)(2,1)S(1)} %bitcast.6) | data formatting | bytes 4194304
  (1 shorter events, 0.0 us)
Async XLA Ops:
  114.7 5.0 %copy-start = (bf16[8,4,2,128,128]{4,3,2,1,0:T(8,128)(2,1)S(1)}, bf16[8,4,2,128,128]{4,3,2,1,0:T(8,128)(2,1)}, u32[]{:S(2)}) copy-start(bf16[8,4,2,128,128]{4,3,2,1,0:T(8,128)(2,1)} %get-tuple-element.5) | copy-start | bytes 6291460

commit v3 on v2

--- a/solution.py
+++ b/solution.py
@@ -247,8 +247,11 @@
     cols = band_columns(spectra, band_bins)
     slots = far_list.shape[3]
     smem = pl.BlockSpec(memory_space=pltpu.SMEM)
-    vmem = pl.BlockSpec(memory_space=pltpu.VMEM)
+    whole = pl.BlockSpec(memory_space=pltpu.VMEM)
     sems = pltpu.SemaphoreType.DMA
+    shard = PIECES * DEPTH * BLOCK * 2
+    result = (2 * 2 * BLK_DEV * BLOCK * ngrp * BLK_DEV + nseg * slots * 2 * BLOCK) * BLOCK * 2
+    vmem = (nseg + ngrp + 4) * shard + result + 2 * 1024 * 1024
     near, far = pl.pallas_call(
         functools.partial(kernel, nseg, ngrp),
         out_shape=(
@@ -257,8 +260,8 @@
             ),
             jax.ShapeDtypeStruct((nseg, slots, 2, BLOCK, BLOCK), jnp.bfloat16),
         ),
-        in_specs=[smem, smem, smem, vmem],
-        out_specs=(vmem, vmem),
+        in_specs=[smem, smem, smem, whole],
+        out_specs=(whole, whole),
         scratch_shapes=[
             pltpu.VMEM((nseg, PIECES, DEPTH, BLOCK), jnp.bfloat16),
             pltpu.VMEM((ngrp, PIECES, DEPTH, BLOCK), jnp.bfloat16),
@@ -270,7 +273,7 @@
             sems,
         ],
         compiler_params=pltpu.CompilerParams(
-            collective_id=0, has_side_effects=True, vmem_limit_bytes=56 * 1024 * 1024
+            collective_id=0, has_side_effects=True, vmem_limit_bytes=vmem
         ),
     )(band_bins, far_list.reshape(nseg, nseg * slots * 3), far_count[0], cols)
     return (near, far[None, None])

time: 121 us -> 116 us (0.959)
  Pallas kernels: 112 us -> 109 us
  local copies, waits for them, and re-layouts: 7.88 us -> 5.77 us
    pallas_call x1, Pallas kernels: 109 us -> 105 us  [body(): pl.pallas_call(functools.partial(kernel, nseg, ngrp), out_shape=(jax.Shap...]
    unnamed x5 -> x9, local copies, waits for them, and re-layouts: 7.2 us -> 5.69 us
where the time goes in v3:
time: 116 us
  Pallas kernels  109 us (94%)
  local copies, waits for them, and re-layouts  5.77 us (5%)
    pallas_call x1, Pallas kernels, body(): pl.pallas_call(functools.partial(kernel, nseg, ngrp), out_shape=(jax.Shap...  105 us
    unnamed x9, local copies, waits for them, and re-layouts  5.69 us
    pallas_call x1, Pallas kernels, band_columns(): pl.pallas_call(whiten_kernel, grid=(BLK_DEV,), out_shape=jax.ShapeDtypeSt...  3.71 us

profile of v3, /device:TPU:0, one launch (start us, length us, event | category | flops | bytes accessed | tf_op | source)
XLA Modules:
  0.0 115.5 jit_solution(16777050428398514093)
XLA Ops:
  0.6 0.0 copy-start.1
  0.6 0.0 copy-start.2
  0.7 0.9 copy.7
  1.6 0.1 copy.8.lists
  1.7 3.7 %shard_map.59 = bf16[2,3,768,128]{3,2,1,0:T(8,128)(2,1)} custom-call(s32[2,2]{1,0:T(2,128)} %bins.3, bf16[8,2,128,384]{3,2,1,0:T(8,128)(2,1)} %spectra.1), custom_call_target="tpu_custom_call" | custom-call | tf_op jit(solution)/shard_map/pallas_call | solution.py:49
  5.4 0.0 copy-done.1
  5.4 0.0 copy-done.2
  5.4 0.0 copy-start
  5.4 1.3 %copy-done = bf16[2,3,768,128]{3,2,1,0:T(8,128)(2,1)S(1)} copy-done((bf16[2,3,768,128]{3,2,1,0:T(8,128)(2,1)S(1)}, bf16[2,3,768,128]{3,2,1,0:T(8,128)(2,1)}, u32[]{:S(2)}) %copy-start) | copy-done | bytes 1179672
  6.6 105.4 %shard_map.60 = (bf16[2,2,384,1536]{3,2,1,0:T(8,128)(2,1)S(1)}, bf16[8,4,2,128,128]{4,3,2,1,0:T(8,128)(2,1)S(1)}) custom-call(s32[2,2]{1,0:T(2,128)S(1)} %copy-done.1, s32[8,96]{1,0:T(8,128)S(1)} %copy.8.lists, s32[8,8]{1,0:T(8,128)S(1)} %bitcast.7, bf16[6,768,128]{2,1,0:T(8,128)(2,1)S(1)} %bitcast.5), custom_call_target="tpu_custom_call" | custom-call | tf_op jit(solution)/shard_map/pallas_call | solution.py:255
  112.0 2.2 %copy.11 = bf16[2,2,384,1536]{3,2,1,0:T(8,128)(2,1)} copy(bf16[2,2,384,1536]{3,2,1,0:T(8,128)(2,1)S(1)} %get-tuple-element.8) | data formatting | bytes 9437184
  114.2 1.3 %copy.12 = bf16[1,1,8,4,2,128,128]{6,5,4,3,2,1,0:T(8,128)(2,1)} copy(bf16[1,1,8,4,2,128,128]{6,5,4,3,2,1,0:T(8,128)(2,1)S(1)} %bitcast.6) | data formatting | bytes 4194304
  (1 shorter events, 0.0 us)
Async XLA Ops:
  0.6 4.7 %copy-start.1 = (s32[2,2]{1,0:T(2,128)S(1)}, s32[2,2]{1,0:T(2,128)}, u32[]{:S(2)}) copy-start(s32[2,2]{1,0:T(2,128)} %bins.3) | copy-start | bytes 52
  0.6 4.7 %copy-start.2 = (s32[1,8,8]{2,1,0:T(8,128)S(1)}, s32[1,8,8]{2,1,0:T(8,128)}, u32[]{:S(2)}) copy-start(s32[1,8,8]{2,1,0:T(8,128)} %param.7) | copy-start | bytes 772
  5.4 1.3 %copy-start = (bf16[2,3,768,128]{3,2,1,0:T(8,128)(2,1)S(1)}, bf16[2,3,768,128]{3,2,1,0:T(8,128)(2,1)}, u32[]{:S(2)}) copy-start(bf16[2,3,768,128]{3,2,1,0:T(8,128)(2,1)} %shard_map.59) | copy-start | bytes 3538948
